TPU v7x, 256 devices: a whole 4x4x8 slice. The times are simulated.
256 devices in a mesh: mp: 4 (over z_lo), proj: 64 (over x, y, z_hi, core).
Axes of the slice: x: 4, y: 4, z: 8 (z_hi: 2, z_lo: 4; z = z_hi * 4 + z_lo), core: 2. Of those that a mesh axis runs over, the one named last changes fastest.
Arguments:
- normed_hidden_input: bfloat16 [8192, 5120], P('proj', 'mp'), may hold values from -6 to 6
- attention_mixture: bfloat16 [8192, 5120], P('proj', 'mp'), may hold values from -6 to 6
- normed_gate_input: bfloat16 [8192, 5120], P('proj', 'mp'), may hold values from -6 to 6
- down_projection_input: bfloat16 [8192, 27648], P('proj', 'mp'), may hold values from -6 to 6
- query_out_cotangent: bfloat16 [8192, 5120], P('proj', 'mp'), may hold values from -6 to 6
- key_value_cotangents: bfloat16 [8192, 2, 1024], P('proj', None, 'mp'), may hold values from -6 to 6
- attention_out_cotangent: bfloat16 [8192, 5120], P('proj', 'mp'), may hold values from -6 to 6
- gate_up_cotangents: bfloat16 [8192, 2, 27648], P('proj', None, 'mp'), may hold values from -6 to 6
- down_out_cotangent: bfloat16 [8192, 5120], P('proj', 'mp'), may hold values from -6 to 6
- adapter_input_factors: bfloat16 [6, 8, 5120], P(None, None, 'mp'), may hold values from -0.078125 to 0.078125
- down_adapter_input_factor: bfloat16 [8, 27648], P(None, 'mp'), may hold values from -0.0390625 to 0.0390625
- adapter_output_factors: bfloat16 [3, 8, 5120], P(None, None, 'mp'), may hold values from -0.078125 to 0.078125
- key_value_adapter_output: bfloat16 [2, 8, 1024], P(None, None, 'mp'), may hold values from -0.1875 to 0.1875
- gate_up_adapter_output: bfloat16 [2, 8, 27648], P(None, None, 'mp'), may hold values from -0.0390625 to 0.0390625
- verified_loss_mask: int32 [8192], P('proj'), may hold values 0 or 1
- block_projector_seeds: int32 [14], replicated, may hold values from 0 to 16777215
Outputs:
- features: float32 [4, 2048], P(None, ('mp', 'proj'))
All inputs are finite; a program needn't handle non-finite values. No bound on the sum of `verified_loss_mask` on one device may be relied on, other than what follows from the above.
Results may differ from a plain program's by a relative error of at most 0.0028.
Values sent between devices are 32-bit elements; how exact they have to be, the bound alone decides.
A program may use at most 64 MiB of HBM per device.

v0:
```python
import math

import jax
import jax.numpy as jnp
from jax import lax
from jax.sharding import PartitionSpec as P

K = 2048
LENGTH = 2048


def mix_bits(row_keys, col_keys):
    hashed = row_keys[:, None] ^ col_keys[None, :]
    hashed = hashed ^ hashed >> 16 & 65535
    hashed = hashed * -2048144789
    hashed = hashed ^ hashed >> 13 & 524287
    hashed = hashed * -1028477387
    hashed = hashed ^ hashed >> 16 & 65535
    byte_sum = (hashed & 255) + (hashed >> 8 & 255) + (hashed >> 16 & 255) + (hashed >> 24 & 255)
    return (byte_sum - 510).astype(jnp.float32)


def project_rows(gradients, row_keys, col_keys, block_limit):
    row_count = gradients.shape[1]
    block_rows = math.gcd(row_count, block_limit)

    def add_block(number, accumulated):
        first_row = (number * block_rows).astype(jnp.int32)
        grad_block = lax.dynamic_slice_in_dim(gradients, first_row, block_rows, 1)
        key_block = lax.dynamic_slice_in_dim(row_keys, first_row, block_rows, 0)
        table = mix_bits(key_block, col_keys)
        return accumulated + jnp.dot(
            grad_block, table, precision=lax.Precision.HIGHEST, preferred_element_type=jnp.float32
        )

    zero_acc = jnp.zeros((gradients.shape[0], col_keys.shape[0]), jnp.float32)
    return lax.fori_loop(0, row_count // block_rows, add_block, zero_acc)


def owned_keys(positions, widths, adapter_rank_count, block_projector_seeds, model_shard):
    key_table = jnp.zeros_like(positions)
    lower_edge = 0
    for segment, seg_width in enumerate(widths):
        upper_edge = lower_edge + adapter_rank_count * seg_width
        offset_pos = positions - lower_edge
        rank_pos = offset_pos // seg_width
        feature = model_shard * seg_width + offset_pos % seg_width
        seg_keys = (
            block_projector_seeds[segment] * 1103515245
            + (feature * adapter_rank_count + rank_pos) * 668265263
        )
        inside = (positions >= lower_edge) & (positions < upper_edge)
        key_table = jnp.where(inside, seg_keys, key_table)
        lower_edge = upper_edge
    return key_table


def shards(
    normed_hidden_input,
    attention_mixture,
    normed_gate_input,
    down_projection_input,
    query_out_cotangent,
    key_value_cotangents,
    attention_out_cotangent,
    gate_up_cotangents,
    down_out_cotangent,
    adapter_input_factors,
    down_adapter_input_factor,
    adapter_output_factors,
    key_value_adapter_output,
    gate_up_adapter_output,
    verified_loss_mask,
    block_projector_seeds,
):
    block_triplets = [
        (
            normed_hidden_input,
            query_out_cotangent,
            adapter_input_factors[0],
            adapter_output_factors[0],
        ),
        (
            normed_hidden_input,
            key_value_cotangents[:, 0],
            adapter_input_factors[1],
            key_value_adapter_output[0],
        ),
        (
            normed_hidden_input,
            key_value_cotangents[:, 1],
            adapter_input_factors[2],
            key_value_adapter_output[1],
        ),
        (
            attention_mixture,
            attention_out_cotangent,
            adapter_input_factors[3],
            adapter_output_factors[1],
        ),
        (
            normed_gate_input,
            gate_up_cotangents[:, 0],
            adapter_input_factors[4],
            gate_up_adapter_output[0],
        ),
        (
            normed_gate_input,
            gate_up_cotangents[:, 1],
            adapter_input_factors[5],
            gate_up_adapter_output[1],
        ),
        (
            down_projection_input,
            down_out_cotangent,
            down_adapter_input_factor,
            adapter_output_factors[2],
        ),
    ]
    factors = []
    for inputs, cotangent, factor_a, factor_b in block_triplets:
        factors.append(
            jnp.einsum("tf,rf->tr", inputs, factor_a, preferred_element_type=jnp.float32)
        )
        factors.append(
            jnp.einsum("tf,rf->tr", cotangent, factor_b, preferred_element_type=jnp.float32)
        )
    summed_factors = lax.psum(jnp.concatenate(factors, axis=1), "mp")
    adapter_rank_count = down_adapter_input_factor.shape[0]
    weights = verified_loss_mask.astype(jnp.float32)[:, None]
    flat_parts = []
    widths = []
    for number, (inputs, cotangent, factor_a, factor_b) in enumerate(block_triplets):
        act_a = summed_factors[
            :, 2 * number * adapter_rank_count : (2 * number + 1) * adapter_rank_count
        ]
        act_b = summed_factors[
            :, (2 * number + 1) * adapter_rank_count : (2 * number + 2) * adapter_rank_count
        ]
        masked_v = (weights * act_a).astype(jnp.bfloat16)
        masked_u = (weights * act_b).astype(jnp.bfloat16)
        grad_a = jnp.einsum("tr,tf->rf", masked_u, inputs, preferred_element_type=jnp.float32)
        grad_b = jnp.einsum("tr,tf->rf", masked_v, cotangent, preferred_element_type=jnp.float32)
        flat_parts.append(grad_a.reshape(-1))
        flat_parts.append(grad_b.reshape(-1))
        widths.append(inputs.shape[1])
        widths.append(cotangent.shape[1])
    local_grads = jnp.concatenate(flat_parts)
    model_shard = lax.axis_index("mp")
    owner_index = lax.axis_index("proj")
    owner_count = lax.axis_size("proj")
    tok_rows = verified_loss_mask.shape[0]
    examples = owner_count * tok_rows // LENGTH
    col_keys = jnp.arange(K, dtype=jnp.int32) * -1640531535
    slice_len = local_grads.shape[0] // owner_count
    received = lax.all_to_all(
        local_grads.reshape(owner_count, slice_len), "proj", split_axis=0, concat_axis=0, tiled=True
    )
    owned_grads = received.reshape(examples, owner_count // examples, slice_len).sum(axis=1)
    positions = owner_index * slice_len + jnp.arange(slice_len, dtype=jnp.int32)
    row_keys = owned_keys(positions, widths, adapter_rank_count, block_projector_seeds, model_shard)
    partial_proj = project_rows(owned_grads, row_keys, col_keys, 1024)
    summed = lax.psum_scatter(partial_proj, ("mp", "proj"), scatter_dimension=1, tiled=True)
    scale_out = 1.0 / (LENGTH * math.sqrt(21845.0 * K))
    return summed * scale_out


def solution(mesh):
    in_specs = (
        P("proj", "mp"),
        P("proj", "mp"),
        P("proj", "mp"),
        P("proj", "mp"),
        P("proj", "mp"),
        P("proj", None, "mp"),
        P("proj", "mp"),
        P("proj", None, "mp"),
        P("proj", "mp"),
        P(None, None, "mp"),
        P(None, "mp"),
        P(None, None, "mp"),
        P(None, None, "mp"),
        P(None, None, "mp"),
        P("proj"),
        P(),
    )
    out_specs = P(None, ("mp", "proj"))
    return jax.shard_map(shards, mesh=mesh, in_specs=in_specs, out_specs=out_specs, check_vma=False)
```

profile of v0, /device:TPU:1, one launch (start us, length us, event | category | flops | bytes accessed | tf_op | source)
XLA Modules:
  0.0 226.3 jit_solution(6597261361760459389)
XLA Ops:
  0.8 1.8 convolution_dynamic-update-slice_fusion.13
  2.6 1.8 convolution_dynamic-update-slice_fusion.12
  4.4 1.8 convolution_dynamic-update-slice_fusion.11
  6.1 1.2 fusion.342
  7.3 1.4 convolution_dynamic-update-slice_fusion.10
  8.8 1.8 convolution_dynamic-update-slice_fusion.9
  10.6 7.7 %fusion.341 = (bf16[128,1,6912]{2,1,0:T(2,128)(2,1)S(1)}, bf16[128,1,6912]{2,1,0:T(2,128)(2,1)S(1)}) fusion(bf16[128,2,6912]{2,1,0:T(2,128)(2,1)} %param.25), kind=kLoop, calls=%fused_computation.424 | loop fusion | bytes 7077888 | tf_op jit(solution)/shard_map/slice | solution.py:109
  19.9 1.3 convolution_dynamic-update-slice_fusion.6
  22.1 1.2 convolution_dynamic-update-slice_fusion.4
  24.0 1.2 convolution_dynamic-update-slice_fusion.2
  25.2 1.2 convolution_dynamic-update-slice_fusion.1
  27.2 19.2 %psum.7 = f32[128,112]{0,1:T(8,128)} all-reduce(f32[128,112]{0,1:T(8,128)} %convolution_dynamic-update-slice_fusion), channel_id=1, replica_groups=mesh['mp'=4,'proj'=64] {'mp'}, use_global_device_ids=true, to_apply=%region_0.0 | all-reduce | flops 14336 | bytes 114688 | tf_op jit(solution)/shard_map/psum | solution.py:128
  46.4 3.1 %fusion.53 = f32[8,6912]{1,0:T(8,128)} fusion(bf16[128,1,6912]{2,1,0:T(2,128)(2,1)} %copy-done.3, f32[128,112]{0,1:T(8,128)} %psum.7, f32[128]{0:T(128)S(1)} %convert_element_type.55), kind=kOutput, calls=%fused_computation.70 | convolution fusion | flops 14157824 | bytes 3764736 | tf_op jit(solution)/shard_map/tr,tf->rf/dot_general | solution.py:143
  49.5 3.1 %fusion.52 = f32[8,6912]{1,0:T(8,128)} fusion(bf16[128,1,6912]{2,1,0:T(2,128)(2,1)} %copy-done.2, f32[128,112]{0,1:T(8,128)} %psum.7, f32[128]{0:T(128)S(1)} %convert_element_type.55), kind=kOutput, calls=%fused_computation.69 | convolution fusion | flops 14157824 | bytes 3764736 | tf_op jit(solution)/shard_map/tr,tf->rf/dot_general | solution.py:143
  64.8 15.8 %all-to-all-start = ((f32[64,1,4096]{2,1,0:T(1,128)}), f32[64,1,4096]{2,1,0:T(1,128)S(1)}, u32[]{:S(2)}, u32[]{:S(2)}) async-start(f32[64,1,4096]{2,1,0:T(1,128)} %bitcast.101), calls=%async_computation | async-start | bytes 2097152 | tf_op jit(solution)/shard_map/all_to_all | solution.py:156
  90.1 19.1 %all-to-all-done = f32[64,1,4096]{2,1,0:T(1,128)S(1)} async-done(((f32[64,1,4096]{2,1,0:T(1,128)}), f32[64,1,4096]{2,1,0:T(1,128)S(1)}, u32[]{:S(2)}, u32[]{:S(2)}) %all-to-all-start) | async-done | bytes 1048608 | tf_op jit(solution)/shard_map/all_to_all | solution.py:156
  109.1 1.6 copy.35
  110.7 1.4 reduce_sum.9
  112.1 37.8 %while.16 = (s32[]{:T(128)}, f32[4,2048]{1,0:T(4,128)S(1)}, f32[4,4096]{1,0:T(4,128)S(1)}, s32[4096]{0:T(1024)S(1)}, s32[]{:T(128)}, /*index=5*/s32[]{:T(128)}, s32[]{:T(128)}, s32[]{:T(128)}) while((s32[]{:T(128)}, f32[4,2048]{1,0:T(4,128)S(1)}, f32[4,4096]{1,0:T(4,128)S(1)}, s32[4096]{0:T(1024)S(1)}, s32[]{:T(128)}, ...), condition=%wide.region_3.4_spmd.clone, body=%wide.region_2.3_spmd.clone.sunk | while | flops 151013376 | bytes 110749 | solution.py:37
  112.2 9.4 %fusion.370 = f32[4,2048]{1,0:T(4,128)S(1)} fusion(s32[2048]{0:T(1024)S(1)} %iota_multiply_fusion.2, s32[1024]{0:T(1024)S(1)} %dynamic_slice.27, f32[4,2048]{1,0:T(4,128)S(1)} %get-tuple-element.215, f32[4,4096]{1,0:T(4,128)S(1)} %get-tuple-element.224, s32[]{:T(128)S(6)} %select_n.490, pred[]{:T(512)S(6)} %compare.9), kind=kOutput, calls=%fused_computation.37.clone.1 | convolution fusion | flops 151011328 | bytes 94213 | tf_op jit(solution)/shard_map/while/body/eval_jaxpr/dot_general | solution.py:32
  121.6 9.4 %fusion.370 = f32[4,2048]{1,0:T(4,128)S(1)} fusion(s32[2048]{0:T(1024)S(1)} %iota_multiply_fusion.2, s32[1024]{0:T(1024)S(1)} %dynamic_slice.27, f32[4,2048]{1,0:T(4,128)S(1)} %get-tuple-element.215, f32[4,4096]{1,0:T(4,128)S(1)} %get-tuple-element.224, s32[]{:T(128)S(6)} %select_n.490, pred[]{:T(512)S(6)} %compare.9), kind=kOutput, calls=%fused_computation.37.clone.1 | convolution fusion | flops 151011328 | bytes 94213 | tf_op jit(solution)/shard_map/while/body/eval_jaxpr/dot_general | solution.py:32
  131.1 9.4 %fusion.370 = f32[4,2048]{1,0:T(4,128)S(1)} fusion(s32[2048]{0:T(1024)S(1)} %iota_multiply_fusion.2, s32[1024]{0:T(1024)S(1)} %dynamic_slice.27, f32[4,2048]{1,0:T(4,128)S(1)} %get-tuple-element.215, f32[4,4096]{1,0:T(4,128)S(1)} %get-tuple-element.224, s32[]{:T(128)S(6)} %select_n.490, pred[]{:T(512)S(6)} %compare.9), kind=kOutput, calls=%fused_computation.37.clone.1 | convolution fusion | flops 151011328 | bytes 94213 | tf_op jit(solution)/shard_map/while/body/eval_jaxpr/dot_general | solution.py:32
  140.5 9.4 %fusion.370 = f32[4,2048]{1,0:T(4,128)S(1)} fusion(s32[2048]{0:T(1024)S(1)} %iota_multiply_fusion.2, s32[1024]{0:T(1024)S(1)} %dynamic_slice.27, f32[4,2048]{1,0:T(4,128)S(1)} %get-tuple-element.215, f32[4,4096]{1,0:T(4,128)S(1)} %get-tuple-element.224, s32[]{:T(128)S(6)} %select_n.490, pred[]{:T(512)S(6)} %compare.9), kind=kOutput, calls=%fused_computation.37.clone.1 | convolution fusion | flops 151011328 | bytes 94213 | tf_op jit(solution)/shard_map/while/body/eval_jaxpr/dot_general | solution.py:32
  149.9 75.7 %all-reduce = f32[4,2048]{1,0:T(4,128)S(1)} all-reduce(f32[4,2048]{1,0:T(4,128)S(1)} %get-tuple-element.137), channel_id=2, replica_groups=mesh['mp'=4,'proj'=64] {'mp','proj'}, use_global_device_ids=true, to_apply=%region_4.5.clone | all-reduce | flops 8192 | bytes 65536
  (106 shorter events, 18.6 us)
Async XLA Ops:
  0.0 25.2 %copy-start = (bf16[128,6912]{1,0:T(8,128)(2,1)S(1)}, bf16[128,6912]{1,0:T(8,128)(2,1)}, u32[]{:S(2)}) copy-start(bf16[128,6912]{1,0:T(8,128)(2,1)} %param.21) | copy-start | bytes 5308420
  7.3 11.0 %copy-start.12 = (bf16[128,1,256]{2,1,0:T(2,128)(2,1)}, bf16[128,1,256]{2,1,0:T(2,128)(2,1)S(1)}, u32[]{:S(2)}) copy-start(bf16[128,1,256]{2,1,0:T(2,128)(2,1)S(1)} %get-tuple-element.165) | copy-start | bytes 196612
  10.6 7.8 %copy-start.23 = (bf16[2,8,256]{2,1,0:T(8,128)(2,1)S(1)}, bf16[2,8,256]{2,1,0:T(8,128)(2,1)}, u32[]{:S(2)}) copy-start(bf16[2,8,256]{2,1,0:T(8,128)(2,1)} %param.30) | copy-start | bytes 24580
  10.6 8.5 %copy-start.7 = (bf16[128,1280]{1,0:T(8,128)(2,1)S(1)}, bf16[128,1280]{1,0:T(8,128)(2,1)}, u32[]{:S(2)}) copy-start(bf16[128,1280]{1,0:T(8,128)(2,1)} %param.19) | copy-start | bytes 983044
  10.6 8.5 %copy-start.18 = (bf16[6,8,1280]{2,1,0:T(8,128)(2,1)S(1)}, bf16[6,8,1280]{2,1,0:T(8,128)(2,1)}, u32[]{:S(2)}) copy-start(bf16[6,8,1280]{2,1,0:T(8,128)(2,1)} %param.27) | copy-start | bytes 368644
  10.6 9.3 %copy-start.6 = (bf16[128,1280]{1,0:T(8,128)(2,1)S(1)}, bf16[128,1280]{1,0:T(8,128)(2,1)}, u32[]{:S(2)}) copy-start(bf16[128,1280]{1,0:T(8,128)(2,1)} %param.24) | copy-start | bytes 983044
  10.6 9.3 %copy-start.21 = (bf16[3,8,1280]{2,1,0:T(8,128)(2,1)S(1)}, bf16[3,8,1280]{2,1,0:T(8,128)(2,1)}, u32[]{:S(2)}) copy-start(bf16[3,8,1280]{2,1,0:T(8,128)(2,1)} %param.29) | copy-start | bytes 184324
  10.6 10.6 %copy-start.4 = (bf16[128,1280]{1,0:T(8,128)(2,1)S(1)}, bf16[128,1280]{1,0:T(8,128)(2,1)}, u32[]{:S(2)}) copy-start(bf16[128,1280]{1,0:T(8,128)(2,1)} %param.20) | copy-start | bytes 983044
  10.6 11.4 %copy-start.22 = (bf16[2,8,6912]{2,1,0:T(8,128)(2,1)S(1)}, bf16[2,8,6912]{2,1,0:T(8,128)(2,1)}, u32[]{:S(2)}) copy-start(bf16[2,8,6912]{2,1,0:T(8,128)(2,1)} %param.31) | copy-start | bytes 663556
  18.3 8.1 %copy-start.2 = (bf16[128,1,6912]{2,1,0:T(2,128)(2,1)}, bf16[128,1,6912]{2,1,0:T(2,128)(2,1)S(1)}, u32[]{:S(2)}) copy-start(bf16[128,1,6912]{2,1,0:T(2,128)(2,1)S(1)} %get-tuple-element.164) | copy-start | bytes 5308420
  18.3 8.1 %copy-start.3 = (bf16[128,1,6912]{2,1,0:T(2,128)(2,1)}, bf16[128,1,6912]{2,1,0:T(2,128)(2,1)S(1)}, u32[]{:S(2)}) copy-start(bf16[128,1,6912]{2,1,0:T(2,128)(2,1)S(1)} %get-tuple-element.163) | copy-start | bytes 5308420
  18.3 6.9 %copy-start.19 = (bf16[8,6912]{1,0:T(8,128)(2,1)S(1)}, bf16[8,6912]{1,0:T(8,128)(2,1)}, u32[]{:S(2)}) copy-start(bf16[8,6912]{1,0:T(8,128)(2,1)} %param.28) | copy-start | bytes 331780
  21.2 5.1 %copy-start.5 = (bf16[128,1280]{1,0:T(8,128)(2,1)S(1)}, bf16[128,1280]{1,0:T(8,128)(2,1)}, u32[]{:S(2)}) copy-start(bf16[128,1280]{1,0:T(8,128)(2,1)} %param.26) | copy-start | bytes 983044
  26.4 29.1 %copy-start.1 = (bf16[128,1280]{1,0:T(8,128)(2,1)S(1)}, bf16[128,1280]{1,0:T(8,128)(2,1)}, u32[]{:S(2)}) copy-start(bf16[128,1280]{1,0:T(8,128)(2,1)} %param.18) | copy-start | bytes 983044
  46.4 6.2 %copy-start.13 = (bf16[128,1,256]{2,1,0:T(2,128)(2,1)S(1)}, bf16[128,1,256]{2,1,0:T(2,128)(2,1)}, u32[]{:S(2)}) copy-start(bf16[128,1,256]{2,1,0:T(2,128)(2,1)} %copy-done.12) | copy-start | bytes 196612
  46.4 6.2 %copy-start.14 = (f32[128,112]{0,1:T(8,128)S(1)}, f32[128,112]{0,1:T(8,128)}, u32[]{:S(2)}) copy-start(f32[128,112]{0,1:T(8,128)} %psum.7) | copy-start | bytes 172036
  46.4 9.4 %copy-start.8 = (bf16[128,1280]{1,0:T(8,128)(2,1)S(1)}, bf16[128,1280]{1,0:T(8,128)(2,1)}, u32[]{:S(2)}) copy-start(bf16[128,1280]{1,0:T(8,128)(2,1)} %param.22) | copy-start | bytes 983044
  53.6 4.1 %copy-start.11 = (f32[8,6912]{1,0:T(8,128)S(1)}, f32[8,6912]{1,0:T(8,128)}, u32[]{:S(2)}) copy-start(f32[8,6912]{1,0:T(8,128)} %fusion.52) | copy-start | bytes 663556
  53.6 4.8 %copy-start.10 = (f32[8,6912]{1,0:T(8,128)S(1)}, f32[8,6912]{1,0:T(8,128)}, u32[]{:S(2)}) copy-start(f32[8,6912]{1,0:T(8,128)} %fusion.53) | copy-start | bytes 663556
  55.1 3.3 %copy-start.17 = (f32[8,1280]{1,0:T(8,128)S(1)}, f32[8,1280]{1,0:T(8,128)}, u32[]{:S(2)}) copy-start(f32[8,1280]{1,0:T(8,128)} %fusion.325) | copy-start | bytes 122884
  55.1 3.3 %copy-start.16 = (f32[8,1280]{1,0:T(8,128)S(1)}, f32[8,1280]{1,0:T(8,128)}, u32[]{:S(2)}) copy-start(f32[8,1280]{1,0:T(8,128)} %fusion.320) | copy-start | bytes 122884
  55.1 3.3 %copy-start.15 = (f32[8,1280]{1,0:T(8,128)S(1)}, f32[8,1280]{1,0:T(8,128)}, u32[]{:S(2)}) copy-start(f32[8,1280]{1,0:T(8,128)} %fusion.317) | copy-start | bytes 122884
  56.5 24.1 %copy-start.20 = (s32[14]{0:T(128)S(1)}, s32[14]{0:T(128)}, u32[]{:S(2)}) copy-start(s32[14]{0:T(128)} %param.33) | copy-start | bytes 172
  64.8 44.4 %all-to-all-start = ((f32[64,1,4096]{2,1,0:T(1,128)}), f32[64,1,4096]{2,1,0:T(1,128)S(1)}, u32[]{:S(2)}, u32[]{:S(2)}) async-start(f32[64,1,4096]{2,1,0:T(1,128)} %bitcast.101), calls=%async_computation | async-start | bytes 2097152 | tf_op jit(solution)/shard_map/all_to_all | solution.py:156
  (1 other events, 1.0 us)
where the time goes:
time: 227 us; the launch traced here: 226 us
  blocking collectives  94.8 us (42%)
  matrix products  65.1 us (29%)
  local copies, waits for them, and re-layouts  19.4 us (9%)
  waiting for transfers between devices  19.1 us (8%)
  starting transfers between devices  15.8 us (7%)
  between operations  8.82 us (4%)
  other arithmetic  3.15 us (1%)
    unnamed x1, blocking collectives  75.7 us
    dot_general x4, matrix products, add_block(): jnp.dot(grad_block, table, precision=lax.Precision.HIGHEST, preferred_ele...  37.7 us
    psum x1, blocking collectives, shards(): summed_factors = lax.psum(jnp.concatenate(factors, axis=1), 'mp')  19.2 us
    all_to_all x1, waiting for transfers between devices, shards(): lax.all_to_all(local_grads.reshape(owner_count, slice_len), 'proj', split...  19.1 us
    all_to_all x1, starting transfers between devices, shards(): lax.all_to_all(local_grads.reshape(owner_count, slice_len), 'proj', split...  15.8 us
    dot_general x7, matrix products, shards(): jnp.einsum('tf,rf->tr', inputs, factor_a, preferred_element_type=jnp.floa...  8.89 us
    dot_general x7, matrix products, shards(): jnp.einsum('tf,rf->tr', cotangent, factor_b, preferred_element_type=jnp.f...  8.46 us
    unnamed x64, local copies, waits for them, and re-layouts  7.84 us
  transfers between devices with their start and end apart: 1, of which 1 were waited for; matrix products, arithmetic and copies ran while one was open for 0% of the time, Pallas kernels for 0%

commit v1 on v0

v1 whole, which is shorter than its diff:
```python
import functools
import math

import jax
import jax.numpy as jnp
from jax import lax
from jax.experimental import pallas as pl
from jax.experimental.pallas import tpu as pltpu
from jax.sharding import PartitionSpec as P

K = 2048
LENGTH = 2048
LANES = 128
MESH = pl.DeviceIdType.MESH
F32, BF16, I32 = jnp.float32, jnp.bfloat16, jnp.int32


def wrap(value):
    return (value + 2**31) % 2**32 - 2**31


M1, M2 = -2048144789, -1028477387
SEED_STEP, ROW_STEP, COL_STEP = 1103515245, 668265263, -1640531535

CHUNKS = (
    ((12, 54), (13, 10)),
    ((8, 10), (9, 54)),
    ((10, 10), (11, 54)),
    ((0, 10), (1, 10), (2, 10), (3, 2), (4, 10), (5, 2), (6, 10), (7, 10)),
)
GROUPS = ((0, 2), (2, 4), (6, 8))
ROWS = 32
STEPS = 4096 // ROWS


def srl(value, count):
    return lax.shift_right_logical(value, jnp.int32(count))


def nt(a, b):
    return lax.dot_general(a, b, (((1,), (1,)), ((), ())), preferred_element_type=F32)


def nn(a, b):
    return jnp.dot(a, b, preferred_element_type=F32)


def kernel(
    xh_in, xo_in, xg_in, xd_in, gq_in, kv_in, go_in, gu_in, gd_in, ai_in, ad_in, ao_in, kvb_in, gub_in, mask_in, seed_in,
    out_ref,
    xh, xo, xg, xd, gq, kv, go, gu, gd, ai, ad, ao, kvb, gub, mask, seed,
    key_base, col_key, table, part, part_in, grads, core_in, half, y_in, quarter, z_in, lhs, total, a_out, a_in, b_in,
    load_sem, mp_send, mp_recv, core_send, core_recv, y_send, y_recv, z_send, z_recv, fin_send, fin_recv,
):
    mp = lax.axis_index("mp")
    proj = lax.axis_index("proj")
    x, y, zh, core = proj // 16, (proj // 4) % 4, (proj // 2) % 2, proj % 2

    def device(x, y, zh, core, mp):
        return {"mp": mp, "proj": x * 16 + y * 4 + zh * 2 + core}

    def turn(value, by, size):
        return (value + by) % size

    plane = [(dx, dy) for dx in range(4) for dy in range(4) if dx or dy]
    column = [(dm, dz, dc) for dm in range(4) for dz in range(2) for dc in range(2) if dm or dz or dc]
    cross = [(dx, dz) for dx in range(4) for dz in range(2) if dx or dz]
    greet = [device(turn(x, dx, 4), turn(y, dy, 4), zh, core, mp) for dx, dy in plane]
    greet += [device(x, y, turn(zh, dz, 2), turn(core, dc, 2), turn(mp, dm, 4)) for dm, dz, dc in column]
    greet += [device(turn(x, dx, 4), y, 1 - zh, core, mp) for dx in range(1, 4)]
    barrier = pltpu.get_barrier_semaphore()
    for peer in greet:
        pl.semaphore_signal(barrier, inc=1, device_id=peer, device_id_type=MESH)

    def load(number, source, target):
        pltpu.make_async_copy(source, target, load_sem.at[number]).start()

    def loaded(number, target):
        pltpu.make_async_copy(target, target, load_sem.at[number]).wait()

    load(15, seed_in, seed)
    load(10, ad_in, ad)
    load(3, xd_in, xd)
    load(11, ao_in, ao)
    load(8, gd_in, gd)
    load(13, gub_in, gub)
    for tile in range(54):
        load(7, gu_in.at[:, :, tile * LANES : (tile + 1) * LANES], gu.at[tile])
    load(9, ai_in, ai)
    load(2, xg_in, xg)
    load(0, xh_in, xh)
    load(12, kvb_in, kvb)
    for tile in range(2):
        load(5, kv_in.at[:, :, tile * LANES : (tile + 1) * LANES], kv.at[tile])
    load(4, gq_in, gq)
    load(1, xo_in, xo)
    load(6, go_in, go)
    load(14, mask_in, mask)

    place = lax.broadcasted_iota(I32, (8, K), 1)
    q, m, i = place >> 7, (place >> 3) & 15, place & 7
    col = (((m >> 2) * 64 + q * 4 + (m & 3)) * 8 + i) * COL_STEP
    col_key[...] = col ^ srl(col, 16)

    loaded(15, seed)
    block = core * 32 + y * 8 + x * 2 + zh
    for chunk, segments in enumerate(CHUNKS):
        edge = 0
        first = jnp.int32(0)
        for segment, blocks in segments:
            here = seed[segment] * SEED_STEP + (mp * blocks + block - edge) * wrap(LANES * 8 * ROW_STEP)
            first = here if edge == 0 else jnp.where(block >= edge, here, first)
            edge += blocks
        for rank in range(8):
            key_base[chunk * 8 + rank] = first + wrap(rank * ROW_STEP)

    def hash_step(step, carry):
        del carry
        base = key_base[step // (LANES // ROWS)]
        row0 = (step % (LANES // ROWS)) * ROWS
        row = base + (lax.broadcasted_iota(I32, (ROWS, LANES), 0) + row0) * wrap(8 * ROW_STEP)
        row = row ^ srl(row, 16)
        at = pl.multiple_of(step * ROWS, ROWS)
        for tile in range(K // LANES):
            lanes = slice(tile * LANES, (tile + 1) * LANES)
            key = jnp.concatenate([col_key[:, lanes]] * (ROWS // 8), axis=0)
            h = (row ^ key) * M1
            h = h ^ srl(h, 13)
            h = h * M2
            h = h ^ srl(h, 16)
            h = (h & 0x00FF00FF) + (srl(h, 8) & 0x00FF00FF)
            h = srl(h * 0x00010001, 16)
            table[pl.ds(at, ROWS), lanes] = (h.astype(F32) - 510.0).astype(BF16)
        return 0

    done = [0]

    def hash_rows(until):
        if until > done[0]:
            lax.fori_loop(done[0], until, hash_step, 0)
            done[0] = until

    pair = lax.broadcasted_iota(I32, (2 * LANES, LANES), 0)
    token = lax.broadcasted_iota(I32, (2 * LANES, LANES), 1)
    pick = [(pair == 2 * token + j).astype(F32).astype(BF16) for j in range(2)]
    odd = (lax.broadcasted_iota(I32, (8, 2 * LANES), 1) & 1) == 1

    def remote(source, target, send, recv, peer):
        pltpu.make_async_remote_copy(
            src_ref=source, dst_ref=target, send_sem=send, recv_sem=recv, device_id=peer, device_id_type=MESH
        ).start()

    def wait_for(ref, sem):
        pltpu.make_async_copy(ref, ref, sem).wait()

    def paired(buffer, tile):
        return jnp.concatenate(
            [buffer.at[tile].reshape(2 * LANES, LANES)[...], buffer.at[tile + 1].reshape(2 * LANES, LANES)[...]], axis=1
        )

    def send_part(group):
        start, size = GROUPS[group]
        for step in range(1, 4):
            remote(
                part.at[pl.ds(start, size)], part_in.at[step - 1, pl.ds(start, size)], mp_send.at[group], mp_recv.at[group],
                device(x, y, zh, core, turn(mp, step, 4)),
            )

    def factor_products(group):
        if group == 0:
            for number, ref in ((10, ad), (3, xd), (11, ao), (8, gd)):
                loaded(number, ref)
            part[0] = nt(ad[...], xd[...])
            part[1] = nt(ao[2], gd[...])
        elif group == 1:
            for number, ref in ((13, gub), (7, gu), (9, ai), (2, xg)):
                loaded(number, ref)
            both = nt(jnp.concatenate([ai[4], ai[5]], axis=0), xg[...])
            part[2] = both[:8]
            part[3] = both[8:]
            acc = jnp.zeros((16, 2 * LANES), F32)
            for tile in range(0, 54, 2):
                lanes = slice(tile * LANES, (tile + 2) * LANES)
                acc += nt(jnp.concatenate([gub[0, :, lanes], gub[1, :, lanes]], axis=0), paired(gu, tile))
            both = jnp.where(odd, acc[8:], acc[:8])
            part[4] = both[:, :LANES]
            part[5] = both[:, LANES:]
        else:
            for number, ref in ((0, xh), (12, kvb), (5, kv), (4, gq), (1, xo), (6, go)):
                loaded(number, ref)
            three = nt(jnp.concatenate([ai[0], ai[1], ai[2]], axis=0), xh[...])
            for j in range(3):
                part[6 + j] = three[8 * j : 8 * j + 8]
            part[9] = nt(ai[3], xo[...])
            part[10] = nt(ao[0], gq[...])
            part[11] = nt(ao[1], go[...])
            acc = nt(jnp.concatenate([kvb[0], kvb[1]], axis=0), paired(kv, 0))
            both = jnp.where(odd, acc[8:], acc[:8])
            part[12] = both[:, :LANES]
            part[13] = both[:, LANES:]
        send_part(group)

    def put(chunk, at, value):
        for tile in range(value.shape[1] // LANES):
            grads[chunk, at + tile] = value[:, tile * LANES : (tile + 1) * LANES]

    def put_wide(chunk, at, left, right):
        for start in range(0, right.shape[1], 1280):
            width = min(1280, right.shape[1] - start)
            put(chunk, at + start // LANES, nn(left, right[:, start : start + width]))

    def send_core(chunk):
        remote(
            grads.at[chunk, pl.ds((1 - core) * 32, 32)], core_in.at[chunk], core_send.at[chunk], core_recv.at[chunk],
            device(x, y, zh, 1 - core, mp),
        )

    def token_sums(group):
        start, size = GROUPS[group]
        region = part_in.at[:, pl.ds(start, size)]
        wait_for(region, mp_recv.at[group])
        if group == 0:
            loaded(14, mask)
        weights = mask[...].astype(F32)

        def tile(number):
            return (part[number] + part_in[0, number]) + (part_in[1, number] + part_in[2, number])

        def masked(number):
            return (weights * tile(number)).astype(BF16)

        def unmix(number):
            mixed = jnp.concatenate([tile(number), tile(number + 1)], axis=1).astype(BF16)
            return [(weights * nn(mixed, pick[j])).astype(BF16) for j in range(2)]

        def mix(values):
            return jnp.concatenate([nt(values[j], pick[j]) for j in range(2)], axis=0).astype(BF16)

        if group == 0:
            v, u = masked(0), masked(1)
            put_wide(0, 0, u, xd)
            put_wide(0, 54, v, gd)
            send_core(0)
        elif group == 1:
            v = mix([masked(2), masked(3)])
            u = jnp.concatenate(unmix(4), axis=0)
            both = nn(u, xg[...])
            put(1, 0, both[:8])
            put(2, 0, both[8:])
            for t in range(0, 54, 2):
                both = nn(v, paired(gu, t))
                put(1, 10 + t, both[:8])
                put(2, 10 + t, both[8:])
            send_core(1)
            send_core(2)
        else:
            vs = [masked(6 + j) for j in range(4)]
            uq, uo = masked(10), masked(11)
            uk, uv = unmix(12)
            three = nn(jnp.concatenate([uq, uk, uv], axis=0), xh[...])
            put(3, 0, three[:8])
            put(3, 10, nn(vs[0], gq[...]))
            put(3, 20, three[8:16])
            put(3, 32, three[16:])
            both = nn(mix([vs[1], vs[2]]), paired(kv, 0))
            put(3, 30, both[:8])
            put(3, 42, both[8:])
            put(3, 44, nn(uo, xo[...]))
            put(3, 54, nn(vs[3], go[...]))
            send_core(3)

    def send_y(chunk):
        wait_for(core_in.at[chunk], core_recv.at[chunk])
        half[chunk] = grads[chunk, pl.ds(core * 32, 32)] + core_in[chunk]
        for step in (2, 1, 3):
            to = turn(y, step, 4)
            remote(
                half.at[chunk, pl.ds(to * 8, 8)], y_in.at[chunk, step - 1], y_send.at[chunk], y_recv.at[chunk],
                device(x, to, zh, core, mp),
            )

    def send_z(chunk):
        wait_for(y_in.at[chunk], y_recv.at[chunk])
        quarter[chunk] = (half[chunk, pl.ds(y * 8, 8)] + y_in[chunk, 0]) + (y_in[chunk, 1] + y_in[chunk, 2])
        for dx, dz in cross[::-1]:
            to_x, to_z = turn(x, dx, 4), turn(zh, dz, 2)
            remote(
                quarter.at[chunk, to_x * 2 + to_z], z_in.at[chunk, x * 2 + zh], z_send.at[chunk], z_recv.at[chunk],
                device(to_x, y, to_z, core, mp),
            )
        z_in[chunk, x * 2 + zh] = quarter[chunk, x * 2 + zh]

    def project(chunk):
        wait_for(z_in.at[chunk, pl.ds(0, 7)], z_recv.at[chunk])
        for example in range(4):
            g = z_in[chunk, 2 * example] + z_in[chunk, 2 * example + 1]
            lhs[chunk, pl.ds(example, 8, stride=8), :] = g
            lhs[chunk, pl.ds(4 + example, 8, stride=8), :] = g - g.astype(BF16).astype(F32)
        left = jnp.concatenate([lhs[chunk, pl.ds(8 * rank, 8), :] for rank in range(8)], axis=1).astype(BF16)
        for start in range(0, K, 512):
            product = nn(left, table[chunk * 1024 : (chunk + 1) * 1024, start : start + 512])
            lanes = slice(start, start + 512)
            if chunk == 0:
                total[:, lanes] = product
            else:
                total[:, lanes] += product

    hash_rows(12)
    pl.semaphore_wait(barrier, len(greet))
    for group in range(3):
        factor_products(group)
    hash_rows(24)
    token_sums(0)
    hash_rows(32)
    token_sums(1)
    send_y(0)
    hash_rows(40)
    send_y(1)
    send_y(2)
    token_sums(2)
    hash_rows(56)
    send_z(0)
    send_y(3)
    hash_rows(72)
    send_z(1)
    send_z(2)
    hash_rows(88)
    send_z(3)
    hash_rows(104)
    project(0)
    hash_rows(STEPS)
    for chunk in range(1, 4):
        project(chunk)

    scale_out = 1.0 / (LENGTH * math.sqrt(21845.0 * K))
    for number in range(16):
        lanes = slice(number * LANES, (number + 1) * LANES)
        a_out[number] = (total[0:4, lanes] + total[4:8, lanes]) * scale_out
    here = x * 4 + y
    for dx, dy in plane[::-1]:
        to_x, to_y = turn(x, dx, 4), turn(y, dy, 4)
        remote(
            a_out.at[to_x * 4 + to_y], a_in.at[here], fin_send.at[0], fin_recv.at[0], device(to_x, to_y, zh, core, mp)
        )
    a_in[here] = a_out[here]
    wait_for(a_in.at[pl.ds(0, 15)], fin_recv.at[0])
    there = mp * 4 + zh * 2 + core
    b_in[there] = jnp.sum(a_in[...], axis=0)
    for dm, dz, dc in column[::-1]:
        remote(
            b_in.at[there], b_in.at[there], fin_send.at[1], fin_recv.at[1],
            device(x, y, turn(zh, dz, 2), turn(core, dc, 2), turn(mp, dm, 4)),
        )
    wait_for(b_in.at[pl.ds(0, 15)], fin_recv.at[1])
    summed = jnp.sum(b_in[...], axis=0)
    out_ref[...] = pltpu.roll(summed, (LANES - there * 8) % LANES, 1)

    for group, (start, size) in enumerate(GROUPS):
        wait_for(part_in.at[:, pl.ds(start, size)], mp_send.at[group])
    for chunk in range(4):
        wait_for(core_in.at[chunk], core_send.at[chunk])
        wait_for(y_in.at[chunk], y_send.at[chunk])
        wait_for(z_in.at[chunk, pl.ds(0, 7)], z_send.at[chunk])
    wait_for(a_in.at[pl.ds(0, 15)], fin_send.at[0])
    wait_for(b_in.at[pl.ds(0, 15)], fin_send.at[1])


def shards(*args):
    args = list(args)
    args[14] = args[14].reshape(1, LANES)

    def like(number):
        return pltpu.VMEM(args[number].shape, args[number].dtype)

    scratch = [like(number) for number in range(15)]
    scratch[5] = pltpu.VMEM((2, LANES, 2, LANES), BF16)
    scratch[7] = pltpu.VMEM((54, LANES, 2, LANES), BF16)
    scratch.append(pltpu.SMEM((14,), I32))
    tile = (8, LANES)
    scratch += [
        pltpu.SMEM((32,), I32),
        pltpu.VMEM((8, K), I32),
        pltpu.VMEM((4096, K), BF16),
        pltpu.VMEM((14, *tile), F32),
        pltpu.VMEM((3, 14, *tile), F32),
        pltpu.VMEM((4, 64, *tile), F32),
        pltpu.VMEM((4, 32, *tile), F32),
        pltpu.VMEM((4, 32, *tile), F32),
        pltpu.VMEM((4, 3, 8, *tile), F32),
        pltpu.VMEM((4, 8, *tile), F32),
        pltpu.VMEM((4, 8, *tile), F32),
        pltpu.VMEM((4, 64, LANES), F32),
        pltpu.VMEM((8, K), F32),
        pltpu.VMEM((16, 4, LANES), F32),
        pltpu.VMEM((16, 4, LANES), F32),
        pltpu.VMEM((16, 4, LANES), F32),
        pltpu.SemaphoreType.DMA((16,)),
        pltpu.SemaphoreType.DMA((3,)),
        pltpu.SemaphoreType.DMA((3,)),
    ]
    scratch += [pltpu.SemaphoreType.DMA((4,)) for _ in range(6)]
    scratch += [pltpu.SemaphoreType.DMA((2,)) for _ in range(2)]
    full = pl.pallas_call(
        kernel,
        out_shape=jax.ShapeDtypeStruct((4, LANES), F32),
        in_specs=[pl.BlockSpec(memory_space=pl.ANY)] * 16,
        out_specs=pl.BlockSpec(memory_space=pltpu.VMEM),
        scratch_shapes=scratch,
        compiler_params=pltpu.CompilerParams(collective_id=0, has_side_effects=True, vmem_limit_bytes=56 * 2**20),
    )(*args)
    return full[:, :8]


def solution(mesh):
    in_specs = (
        P("proj", "mp"), P("proj", "mp"), P("proj", "mp"), P("proj", "mp"), P("proj", "mp"), P("proj", None, "mp"),
        P("proj", "mp"), P("proj", None, "mp"), P("proj", "mp"), P(None, None, "mp"), P(None, "mp"), P(None, None, "mp"),
        P(None, None, "mp"), P(None, None, "mp"), P("proj"), P(),
    )
    return jax.shard_map(shards, mesh=mesh, in_specs=in_specs, out_specs=P(None, ("mp", "proj")), check_vma=False)
```

time: 227 us -> 49.7 us (0.22)
  blocking collectives: 94.8 us -> 0 us
  matrix products: 65.1 us -> 0 us
  Pallas kernels: 0 us -> 48.4 us
  waiting for transfers between devices: 19.1 us -> 0 us
  local copies, waits for them, and re-layouts: 19.4 us -> 1.26 us
  starting transfers between devices: 15.8 us -> 0 us
  between operations: 8.82 us -> 0.01 us
  other arithmetic: 3.15 us -> 0 us
    unnamed x1 -> x0, blocking collectives: 75.7 us -> none
    dot_general x32 -> x0, matrix products: 65.1 us -> none  [the longest x4 37.7 us: add_block(): jnp.dot(grad_block, table, precision=lax.Precision.HIGHEST, preferred_ele...]
    pallas_call x0 -> x1, Pallas kernels: none -> 48.4 us  [shards(): pl.pallas_call(kernel, out_shape=jax.ShapeDtypeStruct((4, LANES), F32), i...]
    psum x1 -> x0, blocking collectives: 19.2 us -> none  [shards(): summed_factors = lax.psum(jnp.concatenate(factors, axis=1), 'mp')]
    all_to_all x1 -> x0, waiting for transfers between devices: 19.1 us -> none  [shards(): lax.all_to_all(local_grads.reshape(owner_count, slice_len), 'proj', split...]
    all_to_all x1 -> x0, starting transfers between devices: 15.8 us -> none  [shards(): lax.all_to_all(local_grads.reshape(owner_count, slice_len), 'proj', split...]
    slice x3 -> x0, local copies, waits for them, and re-layouts: 9.59 us -> none  [the longest x1 7.68 us: shards(): gate_up_cotangents[:, 1]]
    unnamed x64 -> x1, local copies, waits for them, and re-layouts: 7.84 us -> 1.26 us
  transfers between devices with their start and end apart: 1 -> 0, of which waited for: 1 -> 0; matrix products, arithmetic and copies ran while one was open for 0% -> 0% of each run, Pallas kernels for 0% -> 0%
where the time goes in v1:
time: 49.7 us; the launch traced here: 49.6 us
  Pallas kernels  48.4 us (97%)
  local copies, waits for them, and re-layouts  1.26 us (3%)
    pallas_call x1, Pallas kernels, shards(): pl.pallas_call(kernel, out_shape=jax.ShapeDtypeStruct((4, LANES), F32), i...  48.4 us
    unnamed x1, local copies, waits for them, and re-layouts  1.26 us

profile of v1, /device:TPU:1, one launch (start us, length us, event | category | flops | bytes accessed | tf_op | source)
XLA Modules:
  0.0 49.6 jit_solution(11368307591343043127)
XLA Ops:
  0.0 48.4 %shard_map.154 = f32[4,128]{1,0:T(4,128)} custom-call(bf16[128,1280]{1,0:T(8,128)(2,1)} %xh_in.1, bf16[128,1280]{1,0:T(8,128)(2,1)} %xo_in.1, bf16[128,1280]{1,0:T(8,128)(2,1)} %xg_in.1, bf16[128,6912]{1,0:T(8,128)(2,1)} %xd_in.1, bf16[128,1280]{1,0:T(8,128)(2,1)} %gq_in.1, bf16[128,2,256]{2,1,0:T(2,128)(2,1)} %kv_in.1, bf16[128,1280]{1,0:T(8,128)(2,1)} %go_in.1, ...), custom_call_target="tpu_custom_call" | custom-call | tf_op jit(solution)/shard_map/pallas_call | solution.py:403
  48.4 1.3 %copy.18 = f32[4,8]{1,0:T(4,128)} copy(f32[4,8]{1,0:T(4,128)} %bitcast.2) | data formatting | bytes 256

commit v2 on v1

--- a/solution.py
+++ b/solution.py
@@ -23,14 +23,17 @@
 SEED_STEP, ROW_STEP, COL_STEP = 1103515245, 668265263, -1640531535
 
 CHUNKS = (
-    ((12, 54), (13, 10)),
-    ((8, 10), (9, 54)),
-    ((10, 10), (11, 54)),
-    ((0, 10), (1, 10), (2, 10), (3, 2), (4, 10), (5, 2), (6, 10), (7, 10)),
+    ((12, 54, 0, 54), (13, 10, 0, 10)),
+    ((9, 54, 0, 27), (11, 54, 0, 27), (8, 10, 0, 10)),
+    ((9, 54, 27, 27), (11, 54, 27, 27), (10, 10, 0, 10)),
+    tuple((segment, blocks, 0, blocks) for segment, blocks in enumerate((10, 10, 10, 2, 10, 2, 10, 10))),
 )
 GROUPS = ((0, 2), (2, 4), (6, 8))
 ROWS = 32
 STEPS = 4096 // ROWS
+GU_UNROLL = 9
+MIX_LOOP = 0
+MIX = (0, 0, 0, 0)
 
 
 def srl(value, count):
@@ -50,7 +53,7 @@
     out_ref,
     xh, xo, xg, xd, gq, kv, go, gu, gd, ai, ad, ao, kvb, gub, mask, seed,
     key_base, col_key, table, part, part_in, grads, core_in, half, y_in, quarter, z_in, lhs, total, a_out, a_in, b_in,
-    load_sem, mp_send, mp_recv, core_send, core_recv, y_send, y_recv, z_send, z_recv, fin_send, fin_recv,
+    load_sem, mp_send, mp_recv, core_send, core_recv, y_send, y_recv, z_send, z_recv, fin_send, fin_recv, told_sem,
 ):
     mp = lax.axis_index("mp")
     proj = lax.axis_index("proj")
@@ -65,9 +68,10 @@
     plane = [(dx, dy) for dx in range(4) for dy in range(4) if dx or dy]
     column = [(dm, dz, dc) for dm in range(4) for dz in range(2) for dc in range(2) if dm or dz or dc]
     cross = [(dx, dz) for dx in range(4) for dz in range(2) if dx or dz]
-    greet = [device(turn(x, dx, 4), turn(y, dy, 4), zh, core, mp) for dx, dy in plane]
-    greet += [device(x, y, turn(zh, dz, 2), turn(core, dc, 2), turn(mp, dm, 4)) for dm, dz, dc in column]
-    greet += [device(turn(x, dx, 4), y, 1 - zh, core, mp) for dx in range(1, 4)]
+    greet = [device(x, y, zh, core, turn(mp, step, 4)) for step in range(1, 4)]
+    greet += [device(x, turn(y, step, 4), zh, core, mp) for step in range(1, 4)]
+    greet += [device(turn(x, step, 4), y, zh, core, mp) for step in range(1, 4)]
+    greet += [device(x, y, zh, 1 - core, mp), device(x, y, 1 - zh, core, 3 - mp)]
     barrier = pltpu.get_barrier_semaphore()
     for peer in greet:
         pl.semaphore_signal(barrier, inc=1, device_id=peer, device_id_type=MESH)
@@ -107,10 +111,10 @@
     for chunk, segments in enumerate(CHUNKS):
         edge = 0
         first = jnp.int32(0)
-        for segment, blocks in segments:
-            here = seed[segment] * SEED_STEP + (mp * blocks + block - edge) * wrap(LANES * 8 * ROW_STEP)
+        for segment, blocks, begin, count in segments:
+            here = seed[segment] * SEED_STEP + (mp * blocks + begin + block - edge) * wrap(LANES * 8 * ROW_STEP)
             first = here if edge == 0 else jnp.where(block >= edge, here, first)
-            edge += blocks
+            edge += count
         for rank in range(8):
             key_base[chunk * 8 + rank] = first + wrap(rank * ROW_STEP)
 
@@ -127,10 +131,10 @@
             h = (row ^ key) * M1
             h = h ^ srl(h, 13)
             h = h * M2
-            h = h ^ srl(h, 16)
-            h = (h & 0x00FF00FF) + (srl(h, 8) & 0x00FF00FF)
-            h = srl(h * 0x00010001, 16)
-            table[pl.ds(at, ROWS), lanes] = (h.astype(F32) - 510.0).astype(BF16)
+            high = srl(h, 16).astype(jnp.int16)
+            low = h.astype(jnp.int16) ^ high
+            carry8 = lax.shift_right_logical(low, jnp.int16(8)) + lax.shift_right_logical(high, jnp.int16(8))
+            table[pl.ds(at, ROWS), lanes] = (low + high - jnp.int16(255) * carry8 - jnp.int16(510)).astype(BF16)
         return 0
 
     done = [0]
@@ -139,6 +143,11 @@
         if until > done[0]:
             lax.fori_loop(done[0], until, hash_step, 0)
             done[0] = until
+
+    def hash_among(count):
+        for step in range(done[0], done[0] + count):
+            hash_step(step, 0)
+        done[0] += count
 
     pair = lax.broadcasted_iota(I32, (2 * LANES, LANES), 0)
     token = lax.broadcasted_iota(I32, (2 * LANES, LANES), 1)
@@ -178,10 +187,20 @@
             both = nt(jnp.concatenate([ai[4], ai[5]], axis=0), xg[...])
             part[2] = both[:8]
             part[3] = both[8:]
-            acc = jnp.zeros((16, 2 * LANES), F32)
-            for tile in range(0, 54, 2):
-                lanes = slice(tile * LANES, (tile + 2) * LANES)
-                acc += nt(jnp.concatenate([gub[0, :, lanes], gub[1, :, lanes]], axis=0), paired(gu, tile))
+
+            begin = done[0]
+            done[0] += MIX_LOOP * (27 // GU_UNROLL)
+
+            def add(step, acc):
+                for extra in range(MIX_LOOP):
+                    hash_step(begin + step * MIX_LOOP + extra, 0)
+                for pair_at in range(GU_UNROLL):
+                    tile = (step * GU_UNROLL + pair_at) * 2
+                    lanes = pl.ds(pl.multiple_of(tile * LANES, 2 * LANES), 2 * LANES)
+                    acc += nt(jnp.concatenate([gub[0, :, lanes], gub[1, :, lanes]], axis=0), paired(gu, tile))
+                return acc
+
+            acc = lax.fori_loop(0, 27 // GU_UNROLL, add, jnp.zeros((16, 2 * LANES), F32))
             both = jnp.where(odd, acc[8:], acc[:8])
             part[4] = both[:, :LANES]
             part[5] = both[:, LANES:]
@@ -198,7 +217,6 @@
             both = jnp.where(odd, acc[8:], acc[:8])
             part[12] = both[:, :LANES]
             part[13] = both[:, LANES:]
-        send_part(group)
 
     def put(chunk, at, value):
         for tile in range(value.shape[1] // LANES):
@@ -214,6 +232,16 @@
             grads.at[chunk, pl.ds((1 - core) * 32, 32)], core_in.at[chunk], core_send.at[chunk], core_recv.at[chunk],
             device(x, y, zh, 1 - core, mp),
         )
+
+    def send_y(chunk):
+        wait_for(core_in.at[chunk], core_recv.at[chunk])
+        half[chunk] = grads[chunk, pl.ds(core * 32, 32)] + core_in[chunk]
+        for step in (2, 1, 3):
+            to = turn(y, step, 4)
+            remote(
+                half.at[chunk, pl.ds(to * 8, 8)], y_in.at[chunk, step - 1], y_send.at[chunk], y_recv.at[chunk],
+                device(x, to, zh, core, mp),
+            )
 
     def token_sums(group):
         start, size = GROUPS[group]
@@ -221,6 +249,8 @@
         wait_for(region, mp_recv.at[group])
         if group == 0:
             loaded(14, mask)
+            for step in range(1, 4):
+                pl.semaphore_signal(told_sem, inc=1, device_id=device(turn(x, step, 4), y, zh, core, mp), device_id_type=MESH)
         weights = mask[...].astype(F32)
 
         def tile(number):
@@ -238,6 +268,7 @@
 
         if group == 0:
             v, u = masked(0), masked(1)
+            hash_among(MIX[0])
             put_wide(0, 0, u, xd)
             put_wide(0, 54, v, gd)
             send_core(0)
@@ -245,18 +276,26 @@
             v = mix([masked(2), masked(3)])
             u = jnp.concatenate(unmix(4), axis=0)
             both = nn(u, xg[...])
-            put(1, 0, both[:8])
-            put(2, 0, both[8:])
-            for t in range(0, 54, 2):
-                both = nn(v, paired(gu, t))
-                put(1, 10 + t, both[:8])
-                put(2, 10 + t, both[8:])
-            send_core(1)
-            send_core(2)
+            put(1, 54, both[:8])
+            put(2, 54, both[8:])
+            for half in range(2):
+                hash_among(MIX[1 + half])
+                for t in range(0, 28, 2) if half == 0 else range(28, 54, 2):
+                    both = nn(v, paired(gu, t))
+                    for which in range(2):
+                        rows = both[8 * which : 8 * which + 8]
+                        for tile_at in range(2):
+                            at = (t + tile_at) % 27 + 27 * which
+                            put(1 + (t + tile_at) // 27, at, rows[:, tile_at * LANES : (tile_at + 1) * LANES])
+                send_core(1 + half)
+                if half == 0:
+                    send_y(0)
+
         else:
             vs = [masked(6 + j) for j in range(4)]
             uq, uo = masked(10), masked(11)
             uk, uv = unmix(12)
+            hash_among(MIX[3])
             three = nn(jnp.concatenate([uq, uk, uv], axis=0), xh[...])
             put(3, 0, three[:8])
             put(3, 10, nn(vs[0], gq[...]))
@@ -269,18 +308,10 @@
             put(3, 54, nn(vs[3], go[...]))
             send_core(3)
 
-    def send_y(chunk):
-        wait_for(core_in.at[chunk], core_recv.at[chunk])
-        half[chunk] = grads[chunk, pl.ds(core * 32, 32)] + core_in[chunk]
-        for step in (2, 1, 3):
-            to = turn(y, step, 4)
-            remote(
-                half.at[chunk, pl.ds(to * 8, 8)], y_in.at[chunk, step - 1], y_send.at[chunk], y_recv.at[chunk],
-                device(x, to, zh, core, mp),
-            )
-
     def send_z(chunk):
         wait_for(y_in.at[chunk], y_recv.at[chunk])
+        if chunk == 0:
+            pl.semaphore_wait(told_sem, 3)
         quarter[chunk] = (half[chunk, pl.ds(y * 8, 8)] + y_in[chunk, 0]) + (y_in[chunk, 1] + y_in[chunk, 2])
         for dx, dz in cross[::-1]:
             to_x, to_z = turn(x, dx, 4), turn(zh, dz, 2)
@@ -305,32 +336,36 @@
             else:
                 total[:, lanes] += product
 
-    hash_rows(12)
+    hash_rows(16)
+    factor_products(0)
+    factor_products(1)
     pl.semaphore_wait(barrier, len(greet))
-    for group in range(3):
-        factor_products(group)
+    send_part(0)
+    send_part(1)
+    factor_products(2)
     hash_rows(24)
+    send_part(2)
+    hash_rows(40)
     token_sums(0)
-    hash_rows(32)
     token_sums(1)
-    send_y(0)
-    hash_rows(40)
     send_y(1)
+    token_sums(2)
     send_y(2)
-    token_sums(2)
-    hash_rows(56)
+    hash_rows(46)
+    send_y(3)
+    hash_rows(62)
     send_z(0)
-    send_y(3)
-    hash_rows(72)
+    hash_rows(88)
     send_z(1)
     send_z(2)
-    hash_rows(88)
+    hash_rows(96)
     send_z(3)
-    hash_rows(104)
+    hash_rows(120)
     project(0)
-    hash_rows(STEPS)
-    for chunk in range(1, 4):
-        project(chunk)
+    project(1)
+    project(2)
+    hash_rows(128)
+    project(3)
 
     scale_out = 1.0 / (LENGTH * math.sqrt(21845.0 * K))
     for number in range(16):
@@ -400,6 +435,7 @@
     ]
     scratch += [pltpu.SemaphoreType.DMA((4,)) for _ in range(6)]
     scratch += [pltpu.SemaphoreType.DMA((2,)) for _ in range(2)]
+    scratch.append(pltpu.SemaphoreType.REGULAR)
     full = pl.pallas_call(
         kernel,
         out_shape=jax.ShapeDtypeStruct((4, LANES), F32),

time: 49.7 us -> 48.4 us (0.974)
  Pallas kernels: 48.4 us -> 47 us
    pallas_call x1, Pallas kernels: 48.4 us -> 47 us  [shards(): pl.pallas_call(kernel, out_shape=jax.ShapeDtypeStruct((4, LANES), F32), i...]
where the time goes in v2:
time: 48.4 us; the launch traced here: 48.3 us
  Pallas kernels  47 us (97%)
  local copies, waits for them, and re-layouts  1.26 us (3%)
    pallas_call x1, Pallas kernels, shards(): pl.pallas_call(kernel, out_shape=jax.ShapeDtypeStruct((4, LANES), F32), i...  47 us
    unnamed x1, local copies, waits for them, and re-layouts  1.26 us

profile of v2, /device:TPU:1, one launch (start us, length us, event | category | flops | bytes accessed | tf_op | source)
XLA Modules:
  0.0 48.3 jit_solution(13584090065138555563)
XLA Ops:
  0.0 47.0 %shard_map.154 = f32[4,128]{1,0:T(4,128)} custom-call(bf16[128,1280]{1,0:T(8,128)(2,1)} %xh_in.1, bf16[128,1280]{1,0:T(8,128)(2,1)} %xo_in.1, bf16[128,1280]{1,0:T(8,128)(2,1)} %xg_in.1, bf16[128,6912]{1,0:T(8,128)(2,1)} %xd_in.1, bf16[128,1280]{1,0:T(8,128)(2,1)} %gq_in.1, bf16[128,2,256]{2,1,0:T(2,128)(2,1)} %kv_in.1, bf16[128,1280]{1,0:T(8,128)(2,1)} %go_in.1, ...), custom_call_target="tpu_custom_call" | custom-call | tf_op jit(solution)/shard_map/pallas_call | solution.py:439
  47.0 1.3 %copy.18 = f32[4,8]{1,0:T(4,128)} copy(f32[4,8]{1,0:T(4,128)} %bitcast.2) | data formatting | bytes 256

commit v3 on v2

--- a/solution.py
+++ b/solution.py
@@ -29,7 +29,7 @@
     tuple((segment, blocks, 0, blocks) for segment, blocks in enumerate((10, 10, 10, 2, 10, 2, 10, 10))),
 )
 GROUPS = ((0, 2), (2, 4), (6, 8))
-ROWS = 32
+ROWS = 64
 STEPS = 4096 // ROWS
 GU_UNROLL = 9
 MIX_LOOP = 0
@@ -336,35 +336,35 @@
             else:
                 total[:, lanes] += product
 
-    hash_rows(16)
+    hash_rows(8)
     factor_products(0)
     factor_products(1)
     pl.semaphore_wait(barrier, len(greet))
     send_part(0)
     send_part(1)
     factor_products(2)
-    hash_rows(24)
+    hash_rows(12)
     send_part(2)
-    hash_rows(40)
+    hash_rows(20)
     token_sums(0)
     token_sums(1)
     send_y(1)
     token_sums(2)
     send_y(2)
-    hash_rows(46)
+    hash_rows(23)
     send_y(3)
-    hash_rows(62)
+    hash_rows(31)
     send_z(0)
-    hash_rows(88)
+    hash_rows(44)
     send_z(1)
     send_z(2)
-    hash_rows(96)
+    hash_rows(48)
     send_z(3)
-    hash_rows(120)
+    hash_rows(60)
     project(0)
     project(1)
     project(2)
-    hash_rows(128)
+    hash_rows(64)
     project(3)
 
     scale_out = 1.0 / (LENGTH * math.sqrt(21845.0 * K))

time: 48.4 us -> 47.7 us (0.986)
  Pallas kernels: 47 us -> 46.3 us
    pallas_call x1, Pallas kernels: 47 us -> 46.3 us  [shards(): pl.pallas_call(kernel, out_shape=jax.ShapeDtypeStruct((4, LANES), F32), i...]
where the time goes in v3:
time: 47.7 us; the launch traced here: 47.6 us
  Pallas kernels  46.3 us (97%)
  local copies, waits for them, and re-layouts  1.26 us (3%)
    pallas_call x1, Pallas kernels, shards(): pl.pallas_call(kernel, out_shape=jax.ShapeDtypeStruct((4, LANES), F32), i...  46.3 us
    unnamed x1, local copies, waits for them, and re-layouts  1.26 us

profile of v3, /device:TPU:1, one launch (start us, length us, event | category | flops | bytes accessed | tf_op | source)
XLA Modules:
  0.0 47.6 jit_solution(1162598195678132078)
XLA Ops:
  0.0 46.3 %shard_map.154 = f32[4,128]{1,0:T(4,128)} custom-call(bf16[128,1280]{1,0:T(8,128)(2,1)} %xh_in.1, bf16[128,1280]{1,0:T(8,128)(2,1)} %xo_in.1, bf16[128,1280]{1,0:T(8,128)(2,1)} %xg_in.1, bf16[128,6912]{1,0:T(8,128)(2,1)} %xd_in.1, bf16[128,1280]{1,0:T(8,128)(2,1)} %gq_in.1, bf16[128,2,256]{2,1,0:T(2,128)(2,1)} %kv_in.1, bf16[128,1280]{1,0:T(8,128)(2,1)} %go_in.1, ...), custom_call_target="tpu_custom_call" | custom-call | tf_op jit(solution)/shard_map/pallas_call | solution.py:439
  46.3 1.3 %copy.18 = f32[4,8]{1,0:T(4,128)} copy(f32[4,8]{1,0:T(4,128)} %bitcast.2) | data formatting | bytes 256
